TPU v7x, 1024 devices: a whole 4x4x32 slice. The times are simulated.
1024 devices in a mesh: group: 16 (over y, z_hi), inner: 64 (over x, z_lo, core).
Axes of the slice: x: 4, y: 4, z: 32 (z_hi: 4, z_lo: 8; z = z_hi * 8 + z_lo), core: 2. Of those that a mesh axis runs over, the one named last changes fastest.
Arguments:
- tokens: bfloat16 [196608, 8192], P(('group', 'inner')), may hold values from -24 to 24
- weight_codes: bfloat16 [8192, 128], P('inner'), may hold values from -4 to 4
- weight_exp: int32 [64], replicated, may hold values from -9 to -5
- grad_exp: int32 [64], replicated, may hold values from -15 to -9
- recast_exp: int32 [64], replicated, may hold values from 0 to 5
- out_grad: bfloat16 [196608, 128], P(('group', 'inner')), may hold values from -0.0234375 to 0.0234375
Outputs:
- activation: bfloat16 [196608, 128], P(('group', 'inner'))
- grad_sum: float32 [8192, 128], P(('inner', 'group'))
All inputs are finite; a program needn't handle non-finite values.
Results may differ from a plain program's by a relative error of at most 0.0085.
Values may be sent and summed in bfloat16 or wider, within the bound.
A program may use at most 32 MiB of HBM per device.

v0:
```python
import jax
import jax.numpy as jnp
from jax import lax
from jax.sharding import PartitionSpec as P

code_limit = 448.0


def body(tokens, weight_codes, weight_exp, grad_exp, recast_exp, out_grad):
    block = weight_codes.shape[1]
    width = tokens.shape[1]
    weight_rows = jnp.exp2(jnp.repeat(weight_exp, block).astype(jnp.float32))
    gathered = lax.all_gather(weight_codes, "inner", axis=0, tiled=True)
    weight = (gathered.astype(jnp.float32) * weight_rows[:, None]).astype(jnp.bfloat16)
    pre = jnp.dot(tokens, weight, preferred_element_type=jnp.float32)
    sig = jax.nn.sigmoid(pre)
    activation = (pre * sig).astype(jnp.bfloat16)
    delta = (out_grad.astype(jnp.float32) * sig * (1.0 + pre * (1.0 - sig))).astype(jnp.bfloat16)
    partial_grad = lax.dot_general(
        tokens, delta, (((0,), (0,)), ((), ())), preferred_element_type=jnp.float32
    )
    inv_grad = jnp.exp2(-jnp.repeat(grad_exp, block).astype(jnp.float32))
    coded = jnp.clip(partial_grad * inv_grad[:, None], -code_limit, code_limit).astype(jnp.bfloat16)
    inner_count = lax.axis_size("inner")
    group_count = lax.axis_size("group")
    owned = width // inner_count
    final_rows = owned // group_count
    inv_recast_all = jnp.exp2(-jnp.repeat(recast_exp, block).astype(jnp.float32))
    inv_recast = lax.dynamic_slice_in_dim(inv_recast_all, lax.axis_index("inner") * owned, owned, 0)
    back_all = jnp.exp2(jnp.repeat(grad_exp + recast_exp, block).astype(jnp.float32))
    final_start = (lax.axis_index("inner") * group_count + lax.axis_index("group")) * final_rows
    scale_back = lax.dynamic_slice_in_dim(back_all, final_start, final_rows, 0)
    arrived = lax.all_to_all(
        coded.reshape(inner_count, owned, block), "inner", split_axis=0, concat_axis=0, tiled=True
    )
    first = jnp.sum(arrived.astype(jnp.float32), axis=0)
    recoded = jnp.clip(first * inv_recast[:, None], -code_limit, code_limit).astype(jnp.bfloat16)
    pieces = recoded.reshape(group_count, final_rows, block)
    landed = lax.all_to_all(pieces, "group", split_axis=0, concat_axis=0, tiled=True)
    summed = jnp.sum(landed.astype(jnp.float32), axis=0)
    grad_sum = summed * scale_back[:, None]
    return (activation, grad_sum)


def solution(mesh):
    placed = (
        P(("group", "inner"), None),
        P("inner", None),
        P(),
        P(),
        P(),
        P(("group", "inner"), None),
    )
    return jax.shard_map(
        body,
        mesh=mesh,
        in_specs=placed,
        out_specs=(P(("group", "inner"), None), P(("inner", "group"), None)),
        check_vma=False,
    )
```

profile of v0, /device:TPU:1, one launch (start us, length us, event | category | flops | bytes accessed | tf_op | source)
XLA Modules:
  0.0 314.5 jit_solution(9869153135904043731)
XLA Ops:
  7.2 0.0 copy-start
  7.2 0.0 all-gather.2.cloned.1.call-start
  7.2 0.7 all-gather.2.cloned.1.call-update
  7.9 0.9 multiply_exponential_fusion.3
  8.8 0.7 multiply_exponential_fusion
  9.5 0.1 broadcast_bitcast_fusion.3
  9.6 0.0 copy-start.1
  9.6 0.1 broadcast_bitcast_fusion.2
  9.7 140.7 %all-gather.2.cloned.1.call-done = bf16[8192,128]{1,0:T(8,128)(2,1)} async-done(((bf16[128,128]{1,0:T(8,128)(2,1)}), bf16[8192,128]{1,0:T(8,128)(2,1)}) %all-gather.2.cloned.1.call-update) | async-done | bytes 2097168 | tf_op jit(solution)/shard_map/all_gather | solution.py:13
  150.4 0.0 copy-done
  150.4 3.8 %multiply_convert_fusion.5 = (bf16[192,128]{1,0:T(8,128)(2,1)}, f32[192,128]{1,0:T(8,128)S(1)}) fusion(bf16[192,8192]{1,0:T(8,128)(2,1)S(1)} %copy-done, bf16[8192,128]{1,0:T(8,128)(2,1)} %all-gather.2.cloned.1.call-done, f32[8192]{0:T(1024)S(1)} %broadcast_bitcast_fusion.3), kind=kOutput, calls=%fused_computation.11 | convolution fusion | flops 405921792 | bytes 5423104 | tf_op jit(solution)/shard_map/dot_general | solution.py:15
  154.2 0.0 copy-done.1
  154.2 0.9 fusion.4
  155.0 1.9 copy.16
  156.9 7.5 %all-to-all-start = ((bf16[64,128,128]{1,2,0:T(8,128)(2,1)}), bf16[64,128,128]{1,2,0:T(8,128)(2,1)}, u32[]{:S(2)}, u32[]{:S(2)}) async-start(bf16[64,128,128]{1,2,0:T(8,128)(2,1)} %bitcast.24), calls=%async_computation | async-start | bytes 4194304 | tf_op jit(solution)/shard_map/all_to_all | solution.py:33
  164.5 0.1 broadcast_bitcast_fusion.1
  164.6 0.1 dynamic_slice.6
  164.7 0.1 mul.66
  164.7 95.7 %all-to-all-done = bf16[64,128,128]{1,2,0:T(8,128)(2,1)} async-done(((bf16[64,128,128]{1,2,0:T(8,128)(2,1)}), bf16[64,128,128]{1,2,0:T(8,128)(2,1)}, u32[]{:S(2)}, u32[]{:S(2)}) %all-to-all-start) | async-done | bytes 2097184 | tf_op jit(solution)/shard_map/all_to_all | solution.py:33
  260.4 1.9 convert_reduce_fusion
  262.3 0.1 copy.12
  262.4 0.7 fusion.7
  263.1 20.4 %all-to-all-start.1 = ((bf16[16,8,128]{2,1,0:T(8,128)(2,1)}), bf16[16,8,128]{2,1,0:T(8,128)(2,1)S(1)}, u32[]{:S(2)}, u32[]{:S(2)}) async-start(bf16[16,8,128]{2,1,0:T(8,128)(2,1)} %fusion.7), calls=%async_computation.1 | async-start | bytes 65536 | tf_op jit(solution)/shard_map/all_to_all | solution.py:39
  283.5 0.1 broadcast_bitcast_fusion
  283.5 0.1 dynamic_slice.7
  283.6 23.4 %all-to-all-done.1 = bf16[16,8,128]{2,1,0:T(8,128)(2,1)S(1)} async-done(((bf16[16,8,128]{2,1,0:T(8,128)(2,1)}), bf16[16,8,128]{2,1,0:T(8,128)(2,1)S(1)}, u32[]{:S(2)}, u32[]{:S(2)}) %all-to-all-start.1) | async-done | bytes 32800 | tf_op jit(solution)/shard_map/all_to_all | solution.py:39
  307.0 0.7 broadcast_multiply_fusion
  (1 shorter events, 0.0 us)
Async XLA Ops:
  7.2 143.2 %copy-start = (bf16[192,8192]{1,0:T(8,128)(2,1)S(1)}, bf16[192,8192]{1,0:T(8,128)(2,1)}, u32[]{:S(2)}) copy-start(bf16[192,8192]{1,0:T(8,128)(2,1)} %param.6) | copy-start | bytes 9437188
  7.2 143.2 %all-gather.2.cloned.1.call-start = ((), (), s32[]{:S(2)}) async-start(), calls=%async_computation.2 | async-start | bytes 2129920 | tf_op jit(solution)/shard_map/all_gather | solution.py:13
  9.6 144.6 %copy-start.1 = (bf16[192,128]{1,0:T(8,128)(2,1)S(1)}, bf16[192,128]{1,0:T(8,128)(2,1)}, u32[]{:S(2)}) copy-start(bf16[192,128]{1,0:T(8,128)(2,1)} %param.11) | copy-start | bytes 147460
  156.9 103.4 %all-to-all-start = ((bf16[64,128,128]{1,2,0:T(8,128)(2,1)}), bf16[64,128,128]{1,2,0:T(8,128)(2,1)}, u32[]{:S(2)}, u32[]{:S(2)}) async-start(bf16[64,128,128]{1,2,0:T(8,128)(2,1)} %bitcast.24), calls=%async_computation | async-start | bytes 4194304 | tf_op jit(solution)/shard_map/all_to_all | solution.py:33
  263.1 43.9 %all-to-all-start.1 = ((bf16[16,8,128]{2,1,0:T(8,128)(2,1)}), bf16[16,8,128]{2,1,0:T(8,128)(2,1)S(1)}, u32[]{:S(2)}, u32[]{:S(2)}) async-start(bf16[16,8,128]{2,1,0:T(8,128)(2,1)} %fusion.7), calls=%async_computation.1 | async-start | bytes 65536 | tf_op jit(solution)/shard_map/all_to_all | solution.py:39
Sparse Core Ops, SparseCore 0:
  10.7 139.6 all-gather.1
where the time goes:
time: 315 us
  waiting for transfers between devices  260 us (83%)
  starting transfers between devices  28 us (9%)
  between operations  14.1 us (4%)
  other arithmetic  4.89 us (2%)
  matrix products  4.64 us (1%)
    all_gather x1, waiting for transfers between devices, body(): gathered = lax.all_gather(weight_codes, 'inner', axis=0, tiled=True)  141 us
    all_to_all x1, waiting for transfers between devices, body(): lax.all_to_all(coded.reshape(inner_count, owned, block), 'inner', split_a...  95.7 us
    all_to_all x1, waiting for transfers between devices, body(): lax.all_to_all(pieces, 'group', split_axis=0, concat_axis=0, tiled=True)  23.4 us
    all_to_all x1, starting transfers between devices, body(): lax.all_to_all(pieces, 'group', split_axis=0, concat_axis=0, tiled=True)  20.4 us
    all_to_all x1, starting transfers between devices, body(): lax.all_to_all(coded.reshape(inner_count, owned, block), 'inner', split_a...  7.55 us
  transfers between devices with their start and end apart: 3, of which 3 were waited for; matrix products, arithmetic and copies ran while one was open for 1% of the time, Pallas kernels for 0%

commit v1 on v0

v1 whole, which is shorter than its diff:
```python
import jax
import jax.numpy as jnp
from jax import lax
from jax.experimental import pallas as pl
from jax.experimental.pallas import tpu as pltpu
from jax.sharding import PartitionSpec as P

code_limit = 448.0
MESH = pl.DeviceIdType.MESH
NX, NY, NZ, RUN = 4, 4, 32, 8
QB, TOK = 128, 192


def mod(a, n):
    return lax.rem(a + 2 * n, n)


def coords():
    g = lax.axis_index("group")
    i = lax.axis_index("inner")
    return i // 16, g // 4, (g % 4) * RUN + (i // 2) % RUN, i % 2


def dev(x, y, z, c):
    x, y, z = mod(x, NX), mod(y, NY), mod(z, NZ)
    return (y * (NZ // RUN) + z // RUN, (x * RUN + z % RUN) * 2 + c)


def pow2(e):
    return jnp.left_shift(jnp.int32(1), e + 15).astype(jnp.float32) * (2.0**-15)


def block(x, zl, c):
    return (x * RUN + zl) * 2 + c


def kernel(
    tok_hbm, codes_hbm, wexp_hbm, gexp_hbm, rexp_hbm, og_hbm,
    act_out, grad_out,
    tok, codes, og, wexp, gexp, rexp,
    wbuf, act, dt, cod, sibin, xout, xin, zout, zin, pout, pin,
    load_sem, act_sem,
    gz_s, gz_r, gx_s, gx_r, gc_s, gc_r,
    sib_s, sib_r, rx_s, rx_r, rz_s, rz_r, p_s, p_r,
    know1, know2,
):
    x, y, z, c = coords()
    zl = z % RUN
    run0 = z - zl
    even = (x + c) % 2 == 0
    four = jnp.where(even, 4, -4)

    loads = [
        pltpu.make_async_copy(src, dst, load_sem.at[k])
        for k, (src, dst) in enumerate(
            ((codes_hbm, codes), (wexp_hbm, wexp), (gexp_hbm, gexp), (rexp_hbm, rexp), (og_hbm, og), (tok_hbm, tok))
        )
    ]
    for copy in loads:
        copy.start()

    barrier = pltpu.get_barrier_semaphore()
    near = [dev(x, y, z, 1 - c)]
    near += [dev(x + d, y, z, c) for d in (1, 2, 3)]
    near += [dev(x, y + d, z, c) for d in (1, 2, 3)]
    near += [dev(x, y, z + d, c) for d in (1, -1, 2, -2, 3, -3, 4, -4)]
    for who in near:
        pl.semaphore_signal(barrier, inc=1, device_id=who, device_id_type=MESH)

    loads[0].wait()
    loads[1].wait()
    own = codes[...].astype(jnp.float32) * pow2(wexp[block(x, zl, c)])
    wbuf[zl, x, c] = own.astype(jnp.bfloat16)
    pl.semaphore_wait(barrier, len(near))

    def offset(k):
        return jnp.where(k == 6, four, (k // 2 + 1) * (1 - 2 * (k % 2)))

    def origin(k):
        return jnp.where(k == 7, zl, mod(zl - offset(k), RUN))

    def gz(k):
        slot = wbuf.at[zl, x, c]
        return pltpu.make_async_remote_copy(
            src_ref=slot, dst_ref=slot, send_sem=gz_s.at[k], recv_sem=gz_r.at[k],
            device_id=dev(x, y, z + offset(k), c), device_id_type=MESH,
        )

    def gz_wait(k):
        slot = wbuf.at[origin(k), x, c]
        pltpu.make_async_remote_copy(
            src_ref=slot, dst_ref=slot, send_sem=gz_s.at[k], recv_sem=gz_r.at[k],
            device_id=dev(x, y, z + offset(k), c), device_id_type=MESH,
        ).wait_recv()

    def gx(k, d, shift):
        slot = wbuf.at[origin(k), mod(x + shift, NX), c]
        return pltpu.make_async_remote_copy(
            src_ref=slot, dst_ref=slot, send_sem=gx_s.at[k, d - 1], recv_sem=gx_r.at[k, d - 1],
            device_id=dev(x + d, y, z, c), device_id_type=MESH,
        )

    def gc(zs, xs, cs):
        slot = wbuf.at[zs, xs, cs]
        return pltpu.make_async_remote_copy(
            src_ref=slot, dst_ref=slot, send_sem=gc_s.at[zs, xs], recv_sem=gc_r.at[zs, xs],
            device_id=dev(x, y, z, 1 - c), device_id_type=MESH,
        )

    def each(n, f):
        lax.fori_loop(0, n, lambda k, _: (f(k), 0)[1], 0)

    each(7, lambda k: gz(6 - k).start())

    def pass_on(k):
        for d in (2, 1, 3):
            gx(k, d, 0).start()
        gc(origin(k), x, c).start()

    pass_on(jnp.int32(7))

    def arrived_z(k):
        gz_wait(k)
        pass_on(k)

    each(7, arrived_z)

    def arrived_x(k):
        k = lax.rem(k + 7, 8)
        for d in (1, 3, 2):
            gx(k, d, -d).wait_recv()
            gc(origin(k), mod(x - d, NX), c).start()

    each(8, arrived_x)

    for copy in loads[2:]:
        copy.wait()

    for d in (4, -4):
        pl.semaphore_signal(know1, inc=1, device_id=dev(x, y, z + d, c), device_id_type=MESH)

    def arrived_c(k):
        gc(k // NX, k % NX, 1 - c).wait_recv()

    each(32, arrived_c)

    def product(k, acc):
        for xs in range(NX):
            cols = pl.ds(pl.multiple_of((xs * RUN + k) * 256, 256), 256)
            w = wbuf[k, xs].reshape(2 * QB, QB)
            acc += jnp.dot(tok[:, cols], w, preferred_element_type=jnp.float32)
        return acc

    pre = lax.fori_loop(0, RUN, product, jnp.zeros((TOK, QB), jnp.float32))
    sig = jax.nn.sigmoid(pre)
    act[...] = (pre * sig).astype(jnp.bfloat16)
    act_copy = pltpu.make_async_copy(act, act_out, act_sem)
    act_copy.start()
    delta = og[...].astype(jnp.float32) * sig * (1.0 + pre * (1.0 - sig))
    dt[...] = delta.astype(jnp.bfloat16).T

    def place(k):
        return mod(zl + k + 1, RUN)

    def sib(k, side):
        return pltpu.make_async_remote_copy(
            src_ref=cod.at[k, side], dst_ref=sibin.at[k], send_sem=sib_s.at[k], recv_sem=sib_r.at[k],
            device_id=dev(x, y, z, 1 - c), device_id_type=MESH,
        )

    def rx(k, d):
        return pltpu.make_async_remote_copy(
            src_ref=xout.at[k, mod(x + d, NX)], dst_ref=xin.at[k, d - 1], send_sem=rx_s.at[k, d - 1],
            recv_sem=rx_r.at[k, d - 1], device_id=dev(x + d, y, z, c), device_id_type=MESH,
        )

    def rz(k):
        return pltpu.make_async_remote_copy(
            src_ref=zout.at[k], dst_ref=zin.at[k], send_sem=rz_s.at[k], recv_sem=rz_r.at[k],
            device_id=dev(x, y, run0 + place(k), c), device_id_type=MESH,
        )

    def coded(k):
        zs = mod(place(k) + 4, RUN)
        for xs in range(NX):
            cols = pl.ds(pl.multiple_of((xs * RUN + zs) * 256, 256), 256)
            part = jnp.dot(dt[...], tok[:, cols], preferred_element_type=jnp.float32)
            for cs in range(2):
                scaled = part[:, cs * QB:(cs + 1) * QB] * pow2(-gexp[block(xs, zs, cs)])
                cod[k, cs, xs] = jnp.clip(scaled, -code_limit, code_limit).astype(jnp.bfloat16)
        sib(k, 1 - c).start()

    def over_cores(k):
        sib(k, 1 - c).wait_recv()
        for xs in range(NX):
            both = cod[k, c, xs].astype(jnp.float32) + sibin[k, xs].astype(jnp.float32)
            xout[k, xs] = both.astype(jnp.bfloat16)
        for d in (2, 1, 3):
            rx(k, d).start()

    def over_x(k):
        total = xout[k, x].astype(jnp.float32)
        for d in (1, 3, 2):
            rx(k, d).wait_recv()
            total += xin[k, d - 1].astype(jnp.float32)
        zout[k] = total.astype(jnp.bfloat16)

        @pl.when(k < 7)
        def _():
            rz(k).start()

    def stage(k):
        @pl.when(k < 8)
        def _():
            coded(k)

        @pl.when((k >= 1) & (k < 9))
        def _():
            over_cores(k - 1)

        @pl.when(k >= 2)
        def _():
            over_x(k - 2)

    each(10, stage)

    pl.semaphore_wait(know1, 2)
    for d in (8, -8):
        pl.semaphore_signal(know2, inc=1, device_id=dev(x, y, z + d, c), device_id_type=MESH)

    def add_z(k, acc):
        rz(k).wait_recv()
        return acc + zin[k].astype(jnp.float32)

    first = lax.fori_loop(0, 7, add_z, zout[7].astype(jnp.float32))
    zl4 = mod(zl + 4, RUN)
    recoded = jnp.clip(first * pow2(-rexp[block(x, zl4, c)]), -code_limit, code_limit)
    recoded = recoded.astype(jnp.bfloat16).astype(jnp.float32)
    pout[...] = recoded.T.reshape(16, 8, QB)
    pl.semaphore_wait(know2, 2)

    me = lax.axis_index("group")

    def piece(k):
        there = mod(me + k, 16)
        return pltpu.make_async_remote_copy(
            src_ref=pout.at[there], dst_ref=pin.at[k], send_sem=p_s.at[k], recv_sem=p_r.at[k],
            device_id=(there, block(x, zl4, c)), device_id_type=MESH,
        )

    each(16, lambda k: piece(k).start())

    def add_piece(k, acc):
        piece(k).wait_recv()
        return acc + pin[k]

    summed = lax.fori_loop(0, 16, add_piece, jnp.zeros((8, QB), jnp.float32))
    mine = block(x, zl, c)
    grad_out[...] = summed * pow2(gexp[mine] + rexp[mine])

    each(7, lambda k: gz(k).wait_send())

    def sent8(k):
        for d in (1, 2, 3):
            gx(k, d, 0).wait_send()
            rx(k, d).wait_send()
        sib(k, 1 - c).wait_send()

    each(8, sent8)
    each(32, lambda k: gc(k // NX, k % NX, c).wait_send())
    each(7, lambda k: rz(k).wait_send())
    each(16, lambda k: piece(k).wait_send())
    act_copy.wait()


def body(tokens, weight_codes, weight_exp, grad_exp, recast_exp, out_grad):
    bf, f32 = jnp.bfloat16, jnp.float32
    dma, vmem = pltpu.SemaphoreType.DMA, pltpu.VMEM
    return pl.pallas_call(
        kernel,
        name="mlp_block",
        out_shape=(jax.ShapeDtypeStruct((TOK, QB), bf), jax.ShapeDtypeStruct((8, QB), f32)),
        in_specs=[pl.BlockSpec(memory_space=pl.ANY)] * 6,
        out_specs=(pl.BlockSpec(memory_space=pl.ANY), pl.BlockSpec(memory_space=pltpu.VMEM)),
        scratch_shapes=[
            vmem((TOK, 8192), bf), vmem((QB, QB), bf), vmem((TOK, QB), bf),
            pltpu.SMEM((64,), jnp.int32), pltpu.SMEM((64,), jnp.int32), pltpu.SMEM((64,), jnp.int32),
            vmem((RUN, NX, 2, QB, QB), bf), vmem((TOK, QB), bf), vmem((QB, TOK), bf),
            vmem((RUN, 2, NX, QB, QB), bf), vmem((RUN, NX, QB, QB), bf),
            vmem((RUN, NX, QB, QB), bf), vmem((RUN, 3, QB, QB), bf),
            vmem((RUN, QB, QB), bf), vmem((7, QB, QB), bf),
            vmem((16, 8, QB), f32), vmem((16, 8, QB), f32),
            dma((6,)), dma,
            dma((7,)), dma((7,)), dma((8, 3)), dma((8, 3)), dma((8, 4)), dma((8, 4)),
            dma((8,)), dma((8,)), dma((8, 3)), dma((8, 3)), dma((7,)), dma((7,)), dma((16,)), dma((16,)),
            pltpu.SemaphoreType.REGULAR, pltpu.SemaphoreType.REGULAR,
        ],
        compiler_params=pltpu.CompilerParams(
            collective_id=0, has_side_effects=True, vmem_limit_bytes=40 * 2**20
        ),
    )(tokens, weight_codes, weight_exp, grad_exp, recast_exp, out_grad)


def solution(mesh):
    placed = (
        P(("group", "inner"), None),
        P("inner", None),
        P(),
        P(),
        P(),
        P(("group", "inner"), None),
    )
    return jax.shard_map(
        body,
        mesh=mesh,
        in_specs=placed,
        out_specs=(P(("group", "inner"), None), P(("inner", "group"), None)),
        check_vma=False,
    )
```

time: 315 us -> 92.8 us (0.29)
  waiting for transfers between devices: 260 us -> 0 us
  Pallas kernels: 0 us -> 85.2 us
  starting transfers between devices: 28 us -> 0 us
  between operations: 14.1 us -> 0.65 us
  other arithmetic: 4.89 us -> 0 us
  matrix products: 4.64 us -> 0 us
  local copies, waits for them, and re-layouts: 2.51 us -> 6.62 us
    all_gather x1 -> x0, waiting for transfers between devices: 141 us -> none  [body(): gathered = lax.all_gather(weight_codes, 'inner', axis=0, tiled=True)]
    all_to_all x2 -> x0, waiting for transfers between devices: 119 us -> none  [the longest x1 95.7 us: body(): lax.all_to_all(coded.reshape(inner_count, owned, block), 'inner', split_a...]
    pallas_call x0 -> x1, Pallas kernels: none -> 85.2 us  [body(): pl.pallas_call(kernel, name='mlp_block', out_shape=(jax.ShapeDtypeStruct(...]
    all_to_all x2 -> x0, starting transfers between devices: 27.9 us -> none  [the longest x1 20.4 us: body(): lax.all_to_all(pieces, 'group', split_axis=0, concat_axis=0, tiled=True)]
    unnamed x4 -> x14, local copies, waits for them, and re-layouts: 0.01 us -> 6.62 us
    dot_general x2 -> x0, matrix products: 4.64 us -> none  [the longest x1 3.77 us: body(): pre = jnp.dot(tokens, weight, preferred_element_type=jnp.float32)]
  transfers between devices with their start and end apart: 3 -> 0, of which waited for: 3 -> 0; matrix products, arithmetic and copies ran while one was open for 1% -> 0% of each run, Pallas kernels for 0% -> 0%
where the time goes in v1:
time: 92.8 us; the launch traced here: 92.5 us
  Pallas kernels  85.2 us (92%)
  local copies, waits for them, and re-layouts  6.62 us (7%)
    pallas_call x1, Pallas kernels, body(): pl.pallas_call(kernel, name='mlp_block', out_shape=(jax.ShapeDtypeStruct(...  85.2 us
    unnamed x14, local copies, waits for them, and re-layouts  6.62 us

profile of v1, /device:TPU:1, one launch (start us, length us, event | category | flops | bytes accessed | tf_op | source)
XLA Modules:
  0.0 92.5 jit_solution(3603333926450005682)
XLA Ops:
  0.6 0.0 copy-start
  0.6 1.9 %copy-done = bf16[192,8192]{1,0:T(8,128)(2,1)S(1)} copy-done((bf16[192,8192]{1,0:T(8,128)(2,1)S(1)}, bf16[192,8192]{1,0:T(8,128)(2,1)}, u32[]{:S(2)}) %copy-start) | copy-done | bytes 3145752
  2.5 0.0 copy-start.1
  2.5 0.8 copy-done.1
  3.3 0.0 copy-start.2
  3.3 0.8 copy-done.2
  4.1 0.0 copy-start.3
  4.1 0.7 copy-done.3
  4.7 0.0 copy-start.4
  4.7 0.7 copy-done.4
  5.4 0.0 copy-start.5
  5.4 0.7 copy-done.5
  6.0 85.2 %mlp_block.1 = (bf16[192,128]{1,0:T(8,128)(2,1)S(1)}, f32[8,128]{1,0:T(8,128)S(1)}) custom-call(bf16[192,8192]{1,0:T(8,128)(2,1)S(1)} %copy-done, bf16[128,128]{1,0:T(8,128)(2,1)S(1)} %copy-done.2, s32[64]{0:T(128)S(1)} %copy-done.3, s32[64]{0:T(128)S(1)} %copy-done.4, s32[64]{0:T(128)S(1)} %copy-done.5, bf16[192,128]{1,0:T(8,128)(2,1)S(1)} %copy-done.1), custom_call_target="tpu_custom_call" | custom-call | tf_op jit(solution)/shard_map/mlp_block/pallas_call | solution.py:279
  91.2 0.6 copy.10
  91.9 0.6 copy.11
Async XLA Ops:
  0.6 1.9 %copy-start = (bf16[192,8192]{1,0:T(8,128)(2,1)S(1)}, bf16[192,8192]{1,0:T(8,128)(2,1)}, u32[]{:S(2)}) copy-start(bf16[192,8192]{1,0:T(8,128)(2,1)} %tok_hbm.1) | copy-start | bytes 9437188
  2.5 0.8 copy-start.1
  3.3 0.8 copy-start.2
  4.1 0.7 copy-start.3
  4.7 0.7 copy-start.4
  5.4 0.7 copy-start.5

commit v2 on v1

--- a/solution.py
+++ b/solution.py
@@ -40,15 +40,13 @@
     tok, codes, og, wexp, gexp, rexp,
     wbuf, act, dt, cod, sibin, xout, xin, zout, zin, pout, pin,
     load_sem, act_sem,
-    gz_s, gz_r, gx_s, gx_r, gc_s, gc_r,
+    gz_s, gz_r, gx_s, gx_r, gy_s, gy_r, gc_s, gc_r,
     sib_s, sib_r, rx_s, rx_r, rz_s, rz_r, p_s, p_r,
     know1, know2,
 ):
     x, y, z, c = coords()
     zl = z % RUN
     run0 = z - zl
-    even = (x + c) % 2 == 0
-    four = jnp.where(even, 4, -4)
 
     loads = [
         pltpu.make_async_copy(src, dst, load_sem.at[k])
@@ -62,7 +60,7 @@
     barrier = pltpu.get_barrier_semaphore()
     near = [dev(x, y, z, 1 - c)]
     near += [dev(x + d, y, z, c) for d in (1, 2, 3)]
-    near += [dev(x, y + d, z, c) for d in (1, 2, 3)]
+    near += [dev(x, y + d, z, c) for d in (1, 3)]
     near += [dev(x, y, z + d, c) for d in (1, -1, 2, -2, 3, -3, 4, -4)]
     for who in near:
         pl.semaphore_signal(barrier, inc=1, device_id=who, device_id_type=MESH)
@@ -73,33 +71,42 @@
     wbuf[zl, x, c] = own.astype(jnp.bfloat16)
     pl.semaphore_wait(barrier, len(near))
 
-    def offset(k):
-        return jnp.where(k == 6, four, (k // 2 + 1) * (1 - 2 * (k % 2)))
-
-    def origin(k):
-        return jnp.where(k == 7, zl, mod(zl - offset(k), RUN))
-
-    def gz(k):
+    odd = (zl + y) % 2
+    four = jnp.where((x + c) % 2 == 0, 4, -4)
+
+    def origin(k, odd):
+        straight = jnp.where(k == 3, 4, jnp.where(k == 2, -2, 2 * k))
+        crossed = (k // 2 * 2 + 1) * (1 - 2 * (k % 2))
+        return mod(zl + jnp.where(odd == 1, crossed, straight), RUN)
+
+    def gz(n, far, k):
         slot = wbuf.at[zl, x, c]
         return pltpu.make_async_remote_copy(
-            src_ref=slot, dst_ref=slot, send_sem=gz_s.at[k], recv_sem=gz_r.at[k],
-            device_id=dev(x, y, z + offset(k), c), device_id_type=MESH,
+            src_ref=slot, dst_ref=slot, send_sem=gz_s.at[n], recv_sem=gz_r.at[k],
+            device_id=dev(x, y, z + far, c), device_id_type=MESH,
         )
 
     def gz_wait(k):
-        slot = wbuf.at[origin(k), x, c]
+        slot = wbuf.at[origin(k, odd), x, c]
         pltpu.make_async_remote_copy(
             src_ref=slot, dst_ref=slot, send_sem=gz_s.at[k], recv_sem=gz_r.at[k],
-            device_id=dev(x, y, z + offset(k), c), device_id_type=MESH,
+            device_id=dev(x, y, z + 1, c), device_id_type=MESH,
         ).wait_recv()
 
     def gx(k, d, shift):
-        slot = wbuf.at[origin(k), mod(x + shift, NX), c]
+        slot = wbuf.at[origin(k, odd), mod(x + shift, NX), c]
         return pltpu.make_async_remote_copy(
             src_ref=slot, dst_ref=slot, send_sem=gx_s.at[k, d - 1], recv_sem=gx_r.at[k, d - 1],
             device_id=dev(x + d, y, z, c), device_id_type=MESH,
         )
 
+    def gy(k, xs, odd):
+        slot = wbuf.at[origin(k, odd), xs, c]
+        return pltpu.make_async_remote_copy(
+            src_ref=slot, dst_ref=slot, send_sem=gy_s.at[k, xs], recv_sem=gy_r.at[k, xs],
+            device_id=dev(x, y + 1 - 2 * (xs % 2), z, c), device_id_type=MESH,
+        )
+
     def gc(zs, xs, cs):
         slot = wbuf.at[zs, xs, cs]
         return pltpu.make_async_remote_copy(
@@ -110,28 +117,58 @@
     def each(n, f):
         lax.fori_loop(0, n, lambda k, _: (f(k), 0)[1], 0)
 
-    each(7, lambda k: gz(6 - k).start())
-
-    def pass_on(k):
+    from_own = [gz(n, far, k) for n, (far, k) in enumerate(
+        ((1, 1), (-1, 0), (3, 3), (-3, 2), (four, 3), (2, 2), (-2, 1))
+    )]
+
+    @pl.when(odd == 0)
+    def _():
+        for copy in from_own:
+            copy.start()
+
+    @pl.when(odd == 1)
+    def _():
+        gc(zl, x, c).start()
+
+    def arrived_z(k):
+        @pl.when((odd == 1) | (k > 0))
+        def _():
+            gz_wait(k)
+
         for d in (2, 1, 3):
             gx(k, d, 0).start()
-        gc(origin(k), x, c).start()
-
-    pass_on(jnp.int32(7))
-
-    def arrived_z(k):
-        gz_wait(k)
-        pass_on(k)
-
-    each(7, arrived_z)
+
+        @pl.when((odd == 1) | (k > 0))
+        def _():
+            gy(k, x, odd).start()
+
+        gc(origin(k, odd), x, c).start()
 
     def arrived_x(k):
-        k = lax.rem(k + 7, 8)
         for d in (1, 3, 2):
             gx(k, d, -d).wait_recv()
-            gc(origin(k), mod(x - d, NX), c).start()
-
-    each(8, arrived_x)
+            gy(k, mod(x - d, NX), odd).start()
+            gc(origin(k, odd), mod(x - d, NX), c).start()
+
+    def gather(k):
+        @pl.when(k >= 3)
+        def _():
+            arrived_x(k - 3)
+
+        @pl.when(k < 4)
+        def _():
+            arrived_z(k)
+
+    each(7, gather)
+
+    def arrived_y(k):
+        for xs in range(NX):
+            @pl.when((odd == 0) | (k > 0) | (xs != x))
+            def _():
+                gy(k, xs, 1 - odd).wait_recv()
+                gc(origin(k, 1 - odd), xs, c).start()
+
+    each(4, arrived_y)
 
     for copy in loads[2:]:
         copy.wait()
@@ -159,8 +196,14 @@
     delta = og[...].astype(jnp.float32) * sig * (1.0 + pre * (1.0 - sig))
     dt[...] = delta.astype(jnp.bfloat16).T
 
+    up = zl * 2 < RUN
+    short, long = jnp.where(up, zl, 7 - zl), jnp.where(up, 7 - zl, zl)
+
     def place(k):
-        return mod(zl + k + 1, RUN)
+        both = k - (long - short)
+        far = jnp.where(both < 0, long - k, short - both // 2)
+        ahead = up ^ ((both >= 0) & (both % 2 == 1))
+        return zl + jnp.where(ahead, far, -far)
 
     def sib(k, side):
         return pltpu.make_async_remote_copy(
@@ -176,9 +219,16 @@
 
     def rz(k):
         return pltpu.make_async_remote_copy(
-            src_ref=zout.at[k], dst_ref=zin.at[k], send_sem=rz_s.at[k], recv_sem=rz_r.at[k],
+            src_ref=zout.at[k], dst_ref=zin.at[zl], send_sem=rz_s.at[k], recv_sem=rz_r.at[zl],
             device_id=dev(x, y, run0 + place(k), c), device_id_type=MESH,
         )
+
+    def rz_wait(k):
+        there = place(k)
+        pltpu.make_async_remote_copy(
+            src_ref=zout.at[k], dst_ref=zin.at[there], send_sem=rz_s.at[k], recv_sem=rz_r.at[there],
+            device_id=dev(x, y, run0 + there, c), device_id_type=MESH,
+        ).wait_recv()
 
     def coded(k):
         zs = mod(place(k) + 4, RUN)
@@ -218,19 +268,21 @@
         def _():
             over_cores(k - 1)
 
+        @pl.when(k == 2)
+        def _():
+            pl.semaphore_wait(know1, 2)
+            for d in (8, -8):
+                pl.semaphore_signal(know2, inc=1, device_id=dev(x, y, z + d, c), device_id_type=MESH)
+
         @pl.when(k >= 2)
         def _():
             over_x(k - 2)
 
     each(10, stage)
 
-    pl.semaphore_wait(know1, 2)
-    for d in (8, -8):
-        pl.semaphore_signal(know2, inc=1, device_id=dev(x, y, z + d, c), device_id_type=MESH)
-
     def add_z(k, acc):
-        rz(k).wait_recv()
-        return acc + zin[k].astype(jnp.float32)
+        rz_wait(k)
+        return acc + zin[place(k)].astype(jnp.float32)
 
     first = lax.fori_loop(0, 7, add_z, zout[7].astype(jnp.float32))
     zl4 = mod(zl + 4, RUN)
@@ -258,19 +310,31 @@
     mine = block(x, zl, c)
     grad_out[...] = summed * pow2(gexp[mine] + rexp[mine])
 
-    each(7, lambda k: gz(k).wait_send())
+    @pl.when(odd == 0)
+    def _():
+        for copy in from_own:
+            copy.wait_send()
+
+    def sent4(k):
+        for d in (1, 2, 3):
+            gx(k, d, 0).wait_send()
+        for xs in range(NX):
+            @pl.when((odd == 1) | (k > 0) | (xs != x))
+            def _():
+                gy(k, xs, odd).wait_send()
+
+    each(4, sent4)
+    each(32, lambda k: gc(k // NX, k % NX, c).wait_send())
+    act_copy.wait()
 
     def sent8(k):
         for d in (1, 2, 3):
-            gx(k, d, 0).wait_send()
             rx(k, d).wait_send()
         sib(k, 1 - c).wait_send()
 
     each(8, sent8)
-    each(32, lambda k: gc(k // NX, k % NX, c).wait_send())
     each(7, lambda k: rz(k).wait_send())
     each(16, lambda k: piece(k).wait_send())
-    act_copy.wait()
 
 
 def body(tokens, weight_codes, weight_exp, grad_exp, recast_exp, out_grad):
@@ -280,23 +344,23 @@
         kernel,
         name="mlp_block",
         out_shape=(jax.ShapeDtypeStruct((TOK, QB), bf), jax.ShapeDtypeStruct((8, QB), f32)),
-        in_specs=[pl.BlockSpec(memory_space=pl.ANY)] * 6,
-        out_specs=(pl.BlockSpec(memory_space=pl.ANY), pl.BlockSpec(memory_space=pltpu.VMEM)),
+        in_specs=[pl.BlockSpec(memory_space=pltpu.HBM)] * 6,
+        out_specs=(pl.BlockSpec(memory_space=pltpu.HBM), pl.BlockSpec(memory_space=pltpu.VMEM)),
         scratch_shapes=[
             vmem((TOK, 8192), bf), vmem((QB, QB), bf), vmem((TOK, QB), bf),
             pltpu.SMEM((64,), jnp.int32), pltpu.SMEM((64,), jnp.int32), pltpu.SMEM((64,), jnp.int32),
             vmem((RUN, NX, 2, QB, QB), bf), vmem((TOK, QB), bf), vmem((QB, TOK), bf),
             vmem((RUN, 2, NX, QB, QB), bf), vmem((RUN, NX, QB, QB), bf),
             vmem((RUN, NX, QB, QB), bf), vmem((RUN, 3, QB, QB), bf),
-            vmem((RUN, QB, QB), bf), vmem((7, QB, QB), bf),
+            vmem((RUN, QB, QB), bf), vmem((RUN, QB, QB), bf),
             vmem((16, 8, QB), f32), vmem((16, 8, QB), f32),
             dma((6,)), dma,
-            dma((7,)), dma((7,)), dma((8, 3)), dma((8, 3)), dma((8, 4)), dma((8, 4)),
-            dma((8,)), dma((8,)), dma((8, 3)), dma((8, 3)), dma((7,)), dma((7,)), dma((16,)), dma((16,)),
+            dma((7,)), dma((4,)), dma((4, 3)), dma((4, 3)), dma((4, 4)), dma((4, 4)), dma((8, 4)), dma((8, 4)),
+            dma((8,)), dma((8,)), dma((8, 3)), dma((8, 3)), dma((7,)), dma((8,)), dma((16,)), dma((16,)),
             pltpu.SemaphoreType.REGULAR, pltpu.SemaphoreType.REGULAR,
         ],
         compiler_params=pltpu.CompilerParams(
-            collective_id=0, has_side_effects=True, vmem_limit_bytes=40 * 2**20
+            collective_id=0, has_side_effects=True, vmem_limit_bytes=60 * 2**20
         ),
     )(tokens, weight_codes, weight_exp, grad_exp, recast_exp, out_grad)
 

time: 92.8 us -> 82.2 us (0.89)
  the two profiles are of different devices: /device:TPU:1 before, /device:TPU:96 now
where the time goes in v2:
time: 82.2 us; the launch traced here: 82 us
  Pallas kernels  78.7 us (96%)
  local copies, waits for them, and re-layouts  2.69 us (3%)
    pallas_call x1, Pallas kernels, body(): pl.pallas_call(kernel, name='mlp_block', out_shape=(jax.ShapeDtypeStruct(...  78.7 us
    unnamed x2, local copies, waits for them, and re-layouts  2.69 us

profile of v2, /device:TPU:96, one launch (start us, length us, event | category | flops | bytes accessed | tf_op | source)
XLA Modules:
  0.0 82.0 jit_solution(7977457137344052376)
XLA Ops:
  0.6 78.7 %mlp_block.1 = (bf16[192,128]{1,0:T(8,128)(2,1)}, f32[8,128]{1,0:T(8,128)}) custom-call(bf16[192,8192]{1,0:T(8,128)(2,1)} %tok_hbm.1, bf16[128,128]{1,0:T(8,128)(2,1)} %codes_hbm.1, s32[64]{0:T(128)} %wexp_hbm.1, s32[64]{0:T(128)} %gexp_hbm.1, s32[64]{0:T(128)} %rexp_hbm.1, bf16[192,128]{1,0:T(8,128)(2,1)} %og_hbm.1), custom_call_target="tpu_custom_call" | custom-call | tf_op jit(solution)/shard_map/mlp_block/pallas_call | solution.py:343
  79.3 1.4 %copy.10 = bf16[192,128]{1,0:T(8,128)(2,1)} copy(bf16[192,128]{1,0:T(8,128)(2,1)} %get-tuple-element.4) | data formatting | bytes 98304
  80.8 1.3 %copy.11 = f32[8,128]{1,0:T(8,128)} copy(f32[8,128]{1,0:T(8,128)} %get-tuple-element.5) | data formatting | bytes 8192

commit v3 on v2

--- a/solution.py
+++ b/solution.py
@@ -38,8 +38,8 @@
     tok_hbm, codes_hbm, wexp_hbm, gexp_hbm, rexp_hbm, og_hbm,
     act_out, grad_out,
     tok, codes, og, wexp, gexp, rexp,
-    wbuf, act, dt, cod, sibin, xout, xin, zout, zin, pout, pin,
-    load_sem, act_sem,
+    wbuf, dt, cod, sibin, xout, xin, zout, zin, pout, pin,
+    load_sem,
     gz_s, gz_r, gx_s, gx_r, gy_s, gy_r, gc_s, gc_r,
     sib_s, sib_r, rx_s, rx_r, rz_s, rz_r, p_s, p_r,
     know1, know2,
@@ -58,10 +58,12 @@
         copy.start()
 
     barrier = pltpu.get_barrier_semaphore()
-    near = [dev(x, y, z, 1 - c)]
-    near += [dev(x + d, y, z, c) for d in (1, 2, 3)]
-    near += [dev(x, y + d, z, c) for d in (1, 3)]
-    near += [dev(x, y, z + d, c) for d in (1, -1, 2, -2, 3, -3, 4, -4)]
+    near = [dev(x, y, z + d, c) for d in (2, -2)]
+    near += [dev(x + 2, y, z, c)]
+    near += [dev(x, y, z + d, c) for d in (1, -1)]
+    near += [dev(x + d, y, z, c) for d in (1, 3)]
+    near += [dev(x, y + d, z, c) for d in (1, 2, 3)]
+    near += [dev(x, y, z, 1 - c)]
     for who in near:
         pl.semaphore_signal(barrier, inc=1, device_id=who, device_id_type=MESH)
 
@@ -72,15 +74,14 @@
     pl.semaphore_wait(barrier, len(near))
 
     odd = (zl + y) % 2
-    four = jnp.where((x + c) % 2 == 0, 4, -4)
 
     def origin(k, odd):
         straight = jnp.where(k == 3, 4, jnp.where(k == 2, -2, 2 * k))
         crossed = (k // 2 * 2 + 1) * (1 - 2 * (k % 2))
         return mod(zl + jnp.where(odd == 1, crossed, straight), RUN)
 
-    def gz(n, far, k):
-        slot = wbuf.at[zl, x, c]
+    def gz(n, far, k, zs):
+        slot = wbuf.at[zs, x, c]
         return pltpu.make_async_remote_copy(
             src_ref=slot, dst_ref=slot, send_sem=gz_s.at[n], recv_sem=gz_r.at[k],
             device_id=dev(x, y, z + far, c), device_id_type=MESH,
@@ -117,9 +118,11 @@
     def each(n, f):
         lax.fori_loop(0, n, lambda k, _: (f(k), 0)[1], 0)
 
-    from_own = [gz(n, far, k) for n, (far, k) in enumerate(
-        ((1, 1), (-1, 0), (3, 3), (-3, 2), (four, 3), (2, 2), (-2, 1))
-    )]
+    forth = (x + c) % 2 == 0
+    from_own = [gz(n, far, k, zl) for n, (far, k) in enumerate(((2, 2), (-2, 1), (1, 1), (-1, 0)))]
+    above, below = mod(zl + 2, RUN), mod(zl - 2, RUN)
+    passed = [gz(4, -1, 2, above), gz(5, 1, 3, below)]
+    passed_far = gz(6, jnp.where(forth, 2, -2), 3, jnp.where(forth, below, above))
 
     @pl.when(odd == 0)
     def _():
@@ -134,6 +137,22 @@
         @pl.when((odd == 1) | (k > 0))
         def _():
             gz_wait(k)
+
+        @pl.when((odd == 0) & (k == 1))
+        def _():
+            passed[0].start()
+
+            @pl.when(jnp.logical_not(forth))
+            def _():
+                passed_far.start()
+
+        @pl.when((odd == 0) & (k == 2))
+        def _():
+            passed[1].start()
+
+            @pl.when(forth)
+            def _():
+                passed_far.start()
 
         for d in (2, 1, 3):
             gx(k, d, 0).start()
@@ -176,34 +195,36 @@
     for d in (4, -4):
         pl.semaphore_signal(know1, inc=1, device_id=dev(x, y, z + d, c), device_id_type=MESH)
 
-    def arrived_c(k):
-        gc(k // NX, k % NX, 1 - c).wait_recv()
-
-    each(32, arrived_c)
-
     def product(k, acc):
-        for xs in range(NX):
-            cols = pl.ds(pl.multiple_of((xs * RUN + k) * 256, 256), 256)
-            w = wbuf[k, xs].reshape(2 * QB, QB)
+        zs = origin(k % 4, lax.rem(odd + k // 4, 2))
+        for xs in range(NX):
+            gc(zs, xs, 1 - c).wait_recv()
+        for xs in range(NX):
+            cols = pl.ds(pl.multiple_of((xs * RUN + zs) * 256, 256), 256)
+            w = wbuf[zs, xs].reshape(2 * QB, QB)
             acc += jnp.dot(tok[:, cols], w, preferred_element_type=jnp.float32)
         return acc
 
     pre = lax.fori_loop(0, RUN, product, jnp.zeros((TOK, QB), jnp.float32))
     sig = jax.nn.sigmoid(pre)
-    act[...] = (pre * sig).astype(jnp.bfloat16)
-    act_copy = pltpu.make_async_copy(act, act_out, act_sem)
-    act_copy.start()
+    act_out[...] = (pre * sig).astype(jnp.bfloat16)
     delta = og[...].astype(jnp.float32) * sig * (1.0 + pre * (1.0 - sig))
     dt[...] = delta.astype(jnp.bfloat16).T
 
-    up = zl * 2 < RUN
-    short, long = jnp.where(up, zl, 7 - zl), jnp.where(up, 7 - zl, zl)
+    rest = RUN - 1
+    up = zl * 2 < rest
+    top = jnp.minimum(zl, rest - 1)
+    short, long = jnp.where(up, top, rest - 1 - top), jnp.where(up, rest - 1 - top, top)
 
     def place(k):
-        both = k - (long - short)
-        far = jnp.where(both < 0, long - k, short - both // 2)
+        n = k - 1
+        both = n - (long - short)
+        far = jnp.where(both < 0, long - n, short - both // 2)
         ahead = up ^ ((both >= 0) & (both % 2 == 1))
-        return zl + jnp.where(ahead, far, -far)
+        return jnp.where(n < 0, 7 - k, jnp.where(zl < rest, top + jnp.where(ahead, far, -far), n))
+
+    early = zl >= rest
+    mine_at = jnp.where(early, 7 - zl, 7)
 
     def sib(k, side):
         return pltpu.make_async_remote_copy(
@@ -223,15 +244,14 @@
             device_id=dev(x, y, run0 + place(k), c), device_id_type=MESH,
         )
 
-    def rz_wait(k):
-        there = place(k)
+    def rz_wait(there):
         pltpu.make_async_remote_copy(
-            src_ref=zout.at[k], dst_ref=zin.at[there], send_sem=rz_s.at[k], recv_sem=rz_r.at[there],
+            src_ref=zout.at[0], dst_ref=zin.at[there], send_sem=rz_s.at[0], recv_sem=rz_r.at[there],
             device_id=dev(x, y, run0 + there, c), device_id_type=MESH,
         ).wait_recv()
 
     def coded(k):
-        zs = mod(place(k) + 4, RUN)
+        zs = 7 - place(k)
         for xs in range(NX):
             cols = pl.ds(pl.multiple_of((xs * RUN + zs) * 256, 256), 256)
             part = jnp.dot(dt[...], tok[:, cols], preferred_element_type=jnp.float32)
@@ -255,7 +275,7 @@
             total += xin[k, d - 1].astype(jnp.float32)
         zout[k] = total.astype(jnp.bfloat16)
 
-        @pl.when(k < 7)
+        @pl.when(place(k) != zl)
         def _():
             rz(k).start()
 
@@ -278,29 +298,39 @@
         def _():
             over_x(k - 2)
 
-    each(10, stage)
-
-    def add_z(k, acc):
-        rz_wait(k)
-        return acc + zin[place(k)].astype(jnp.float32)
-
-    first = lax.fori_loop(0, 7, add_z, zout[7].astype(jnp.float32))
-    zl4 = mod(zl + 4, RUN)
-    recoded = jnp.clip(first * pow2(-rexp[block(x, zl4, c)]), -code_limit, code_limit)
-    recoded = recoded.astype(jnp.bfloat16).astype(jnp.float32)
-    pout[...] = recoded.T.reshape(16, 8, QB)
-    pl.semaphore_wait(know2, 2)
-
-    me = lax.axis_index("group")
+    mirror = 7 - zl
 
     def piece(k):
-        there = mod(me + k, 16)
+        dy = jnp.where(k % 4 == 0, 2, jnp.where(k % 4 == 3, 0, 2 * (k % 4) - 1))
+        side = jnp.where(zl < 4, 1, 3)
+        dz = jnp.where(k // 4 == 0, 2, jnp.where(k // 4 == 1, side, jnp.where(k // 4 == 2, 0, 4 - side)))
+        there = mod(y + dy, NY) * 4 + mod(z // RUN + dz, 4)
         return pltpu.make_async_remote_copy(
             src_ref=pout.at[there], dst_ref=pin.at[k], send_sem=p_s.at[k], recv_sem=p_r.at[k],
-            device_id=(there, block(x, zl4, c)), device_id_type=MESH,
-        )
-
-    each(16, lambda k: piece(k).start())
+            device_id=(there, block(x, mirror, c)), device_id_type=MESH,
+        )
+
+    def over_run():
+        def add_z(k, acc):
+            there = lax.rem(zl + 1 + k, RUN)
+            rz_wait(there)
+            return acc + zin[there].astype(jnp.float32)
+
+        first = lax.fori_loop(0, 7, add_z, zout[mine_at].astype(jnp.float32))
+        recoded = jnp.clip(first * pow2(-rexp[block(x, mirror, c)]), -code_limit, code_limit)
+        recoded = recoded.astype(jnp.bfloat16).astype(jnp.float32)
+        pout[...] = recoded.T.reshape(16, 8, QB)
+        pl.semaphore_wait(know2, 2)
+        each(16, lambda k: piece(k).start())
+
+    def step(k):
+        stage(k)
+
+        @pl.when(k == jnp.where(early, 8, 9))
+        def _():
+            over_run()
+
+    each(10, step)
 
     def add_piece(k, acc):
         piece(k).wait_recv()
@@ -312,7 +342,7 @@
 
     @pl.when(odd == 0)
     def _():
-        for copy in from_own:
+        for copy in from_own + passed + [passed_far]:
             copy.wait_send()
 
     def sent4(k):
@@ -325,7 +355,6 @@
 
     each(4, sent4)
     each(32, lambda k: gc(k // NX, k % NX, c).wait_send())
-    act_copy.wait()
 
     def sent8(k):
         for d in (1, 2, 3):
@@ -333,7 +362,13 @@
         sib(k, 1 - c).wait_send()
 
     each(8, sent8)
-    each(7, lambda k: rz(k).wait_send())
+
+    def sent_z(k):
+        @pl.when(place(k) != zl)
+        def _():
+            rz(k).wait_send()
+
+    each(8, sent_z)
     each(16, lambda k: piece(k).wait_send())
 
 
@@ -343,20 +378,20 @@
     return pl.pallas_call(
         kernel,
         name="mlp_block",
-        out_shape=(jax.ShapeDtypeStruct((TOK, QB), bf), jax.ShapeDtypeStruct((8, QB), f32)),
+        out_shape=(vmem((TOK, QB), bf), vmem((8, QB), f32)),
         in_specs=[pl.BlockSpec(memory_space=pltpu.HBM)] * 6,
-        out_specs=(pl.BlockSpec(memory_space=pltpu.HBM), pl.BlockSpec(memory_space=pltpu.VMEM)),
+        out_specs=(pl.BlockSpec(memory_space=pltpu.VMEM), pl.BlockSpec(memory_space=pltpu.VMEM)),
         scratch_shapes=[
             vmem((TOK, 8192), bf), vmem((QB, QB), bf), vmem((TOK, QB), bf),
             pltpu.SMEM((64,), jnp.int32), pltpu.SMEM((64,), jnp.int32), pltpu.SMEM((64,), jnp.int32),
-            vmem((RUN, NX, 2, QB, QB), bf), vmem((TOK, QB), bf), vmem((QB, TOK), bf),
+            vmem((RUN, NX, 2, QB, QB), bf), vmem((QB, TOK), bf),
             vmem((RUN, 2, NX, QB, QB), bf), vmem((RUN, NX, QB, QB), bf),
             vmem((RUN, NX, QB, QB), bf), vmem((RUN, 3, QB, QB), bf),
             vmem((RUN, QB, QB), bf), vmem((RUN, QB, QB), bf),
             vmem((16, 8, QB), f32), vmem((16, 8, QB), f32),
-            dma((6,)), dma,
+            dma((6,)),
             dma((7,)), dma((4,)), dma((4, 3)), dma((4, 3)), dma((4, 4)), dma((4, 4)), dma((8, 4)), dma((8, 4)),
-            dma((8,)), dma((8,)), dma((8, 3)), dma((8, 3)), dma((7,)), dma((8,)), dma((16,)), dma((16,)),
+            dma((8,)), dma((8,)), dma((8, 3)), dma((8, 3)), dma((8,)), dma((8,)), dma((16,)), dma((16,)),
             pltpu.SemaphoreType.REGULAR, pltpu.SemaphoreType.REGULAR,
         ],
         compiler_params=pltpu.CompilerParams(

time: 82.2 us -> 78 us (0.949)
  the two profiles are of different devices: /device:TPU:96 before, /device:TPU:32 now
where the time goes in v3:
time: 78 us; the launch traced here: 77.9 us
  Pallas kernels  76 us (97%)
  local copies, waits for them, and re-layouts  1.21 us (2%)
    pallas_call x1, Pallas kernels, body(): pl.pallas_call(kernel, name='mlp_block', out_shape=(vmem((TOK, QB), bf),...  76 us

profile of v3, /device:TPU:32, one launch (start us, length us, event | category | flops | bytes accessed | tf_op | source)
XLA Modules:
  0.0 77.9 jit_solution(8584927397927720853)
XLA Ops:
  0.6 76.0 %mlp_block.1 = (bf16[192,128]{1,0:T(8,128)(2,1)S(1)}, f32[8,128]{1,0:T(8,128)S(1)}) custom-call(bf16[192,8192]{1,0:T(8,128)(2,1)} %tok_hbm.1, bf16[128,128]{1,0:T(8,128)(2,1)} %codes_hbm.1, s32[64]{0:T(128)} %wexp_hbm.1, s32[64]{0:T(128)} %gexp_hbm.1, s32[64]{0:T(128)} %rexp_hbm.1, bf16[192,128]{1,0:T(8,128)(2,1)} %og_hbm.1), custom_call_target="tpu_custom_call" | custom-call | tf_op jit(solution)/shard_map/mlp_block/pallas_call | solution.py:378
  76.6 0.6 copy.10
  77.3 0.6 copy.11

commit v4 on v3

--- a/solution.py
+++ b/solution.py
@@ -42,11 +42,10 @@
     load_sem,
     gz_s, gz_r, gx_s, gx_r, gy_s, gy_r, gc_s, gc_r,
     sib_s, sib_r, rx_s, rx_r, rz_s, rz_r, p_s, p_r,
-    know1, know2,
+    know0, know1, know2,
 ):
     x, y, z, c = coords()
     zl = z % RUN
-    run0 = z - zl
 
     loads = [
         pltpu.make_async_copy(src, dst, load_sem.at[k])
@@ -73,6 +72,11 @@
     wbuf[zl, x, c] = own.astype(jnp.bfloat16)
     pl.semaphore_wait(barrier, len(near))
 
+    group, inner = lax.axis_index("group"), lax.axis_index("inner")
+    other = (group, inner + 1 - 2 * c)
+    along_x = {d: dev(x + d, y, z, c) for d in (1, 2, 3)}
+    up_y, down_y = dev(x, y + 1, z, c)[0], dev(x, y - 1, z, c)[0]
+
     odd = (zl + y) % 2
 
     def origin(k, odd):
@@ -91,28 +95,28 @@
         slot = wbuf.at[origin(k, odd), x, c]
         pltpu.make_async_remote_copy(
             src_ref=slot, dst_ref=slot, send_sem=gz_s.at[k], recv_sem=gz_r.at[k],
-            device_id=dev(x, y, z + 1, c), device_id_type=MESH,
+            device_id=other, device_id_type=MESH,
         ).wait_recv()
 
     def gx(k, d, shift):
         slot = wbuf.at[origin(k, odd), mod(x + shift, NX), c]
         return pltpu.make_async_remote_copy(
             src_ref=slot, dst_ref=slot, send_sem=gx_s.at[k, d - 1], recv_sem=gx_r.at[k, d - 1],
-            device_id=dev(x + d, y, z, c), device_id_type=MESH,
+            device_id=along_x[d], device_id_type=MESH,
         )
 
     def gy(k, xs, odd):
         slot = wbuf.at[origin(k, odd), xs, c]
         return pltpu.make_async_remote_copy(
             src_ref=slot, dst_ref=slot, send_sem=gy_s.at[k, xs], recv_sem=gy_r.at[k, xs],
-            device_id=dev(x, y + 1 - 2 * (xs % 2), z, c), device_id_type=MESH,
+            device_id=(jnp.where(xs % 2 == 0, up_y, down_y), inner), device_id_type=MESH,
         )
 
     def gc(zs, xs, cs):
         slot = wbuf.at[zs, xs, cs]
         return pltpu.make_async_remote_copy(
             src_ref=slot, dst_ref=slot, send_sem=gc_s.at[zs, xs], recv_sem=gc_r.at[zs, xs],
-            device_id=dev(x, y, z, 1 - c), device_id_type=MESH,
+            device_id=other, device_id_type=MESH,
         )
 
     def each(n, f):
@@ -179,6 +183,8 @@
             arrived_z(k)
 
     each(7, gather)
+    for d in (4, -4):
+        pl.semaphore_signal(know0, inc=1, device_id=dev(x, y, z + d, c), device_id_type=MESH)
 
     def arrived_y(k):
         for xs in range(NX):
@@ -229,25 +235,25 @@
     def sib(k, side):
         return pltpu.make_async_remote_copy(
             src_ref=cod.at[k, side], dst_ref=sibin.at[k], send_sem=sib_s.at[k], recv_sem=sib_r.at[k],
-            device_id=dev(x, y, z, 1 - c), device_id_type=MESH,
+            device_id=other, device_id_type=MESH,
         )
 
     def rx(k, d):
         return pltpu.make_async_remote_copy(
             src_ref=xout.at[k, mod(x + d, NX)], dst_ref=xin.at[k, d - 1], send_sem=rx_s.at[k, d - 1],
-            recv_sem=rx_r.at[k, d - 1], device_id=dev(x + d, y, z, c), device_id_type=MESH,
+            recv_sem=rx_r.at[k, d - 1], device_id=along_x[d], device_id_type=MESH,
         )
 
     def rz(k):
         return pltpu.make_async_remote_copy(
             src_ref=zout.at[k], dst_ref=zin.at[zl], send_sem=rz_s.at[k], recv_sem=rz_r.at[zl],
-            device_id=dev(x, y, run0 + place(k), c), device_id_type=MESH,
+            device_id=(group, block(x, place(k), c)), device_id_type=MESH,
         )
 
     def rz_wait(there):
         pltpu.make_async_remote_copy(
             src_ref=zout.at[0], dst_ref=zin.at[there], send_sem=rz_s.at[0], recv_sem=rz_r.at[there],
-            device_id=dev(x, y, run0 + there, c), device_id_type=MESH,
+            device_id=other, device_id_type=MESH,
         ).wait_recv()
 
     def coded(k):
@@ -279,24 +285,16 @@
         def _():
             rz(k).start()
 
-    def stage(k):
+    def front(k):
         @pl.when(k < 8)
         def _():
             coded(k)
 
-        @pl.when((k >= 1) & (k < 9))
-        def _():
-            over_cores(k - 1)
-
-        @pl.when(k == 2)
-        def _():
-            pl.semaphore_wait(know1, 2)
-            for d in (8, -8):
-                pl.semaphore_signal(know2, inc=1, device_id=dev(x, y, z + d, c), device_id_type=MESH)
-
-        @pl.when(k >= 2)
-        def _():
-            over_x(k - 2)
+        @pl.when(k >= 4)
+        def _():
+            over_cores(k - 4)
+
+    each(12, front)
 
     mirror = 7 - zl
 
@@ -323,22 +321,24 @@
         pl.semaphore_wait(know2, 2)
         each(16, lambda k: piece(k).start())
 
-    def step(k):
-        stage(k)
-
-        @pl.when(k == jnp.where(early, 8, 9))
+    def back(k):
+        @pl.when(k == 0)
+        def _():
+            pl.semaphore_wait(know0, 2)
+
+        @pl.when(k == 2)
+        def _():
+            pl.semaphore_wait(know1, 2)
+            for d in (8, -8):
+                pl.semaphore_signal(know2, inc=1, device_id=dev(x, y, z + d, c), device_id_type=MESH)
+
+        over_x(k)
+
+        @pl.when(k == jnp.where(early, 7, 7))
         def _():
             over_run()
 
-    each(10, step)
-
-    def add_piece(k, acc):
-        piece(k).wait_recv()
-        return acc + pin[k]
-
-    summed = lax.fori_loop(0, 16, add_piece, jnp.zeros((8, QB), jnp.float32))
-    mine = block(x, zl, c)
-    grad_out[...] = summed * pow2(gexp[mine] + rexp[mine])
+    each(8, back)
 
     @pl.when(odd == 0)
     def _():
@@ -370,6 +370,14 @@
 
     each(8, sent_z)
     each(16, lambda k: piece(k).wait_send())
+
+    def add_piece(k, acc):
+        piece(k).wait_recv()
+        return acc + pin[k]
+
+    summed = lax.fori_loop(0, 16, add_piece, jnp.zeros((8, QB), jnp.float32))
+    mine = block(x, zl, c)
+    grad_out[...] = summed * pow2(gexp[mine] + rexp[mine])
 
 
 def body(tokens, weight_codes, weight_exp, grad_exp, recast_exp, out_grad):
@@ -392,7 +400,7 @@
             dma((6,)),
             dma((7,)), dma((4,)), dma((4, 3)), dma((4, 3)), dma((4, 4)), dma((4, 4)), dma((8, 4)), dma((8, 4)),
             dma((8,)), dma((8,)), dma((8, 3)), dma((8, 3)), dma((8,)), dma((8,)), dma((16,)), dma((16,)),
-            pltpu.SemaphoreType.REGULAR, pltpu.SemaphoreType.REGULAR,
+            pltpu.SemaphoreType.REGULAR, pltpu.SemaphoreType.REGULAR, pltpu.SemaphoreType.REGULAR,
         ],
         compiler_params=pltpu.CompilerParams(
             collective_id=0, has_side_effects=True, vmem_limit_bytes=60 * 2**20

time: 78 us -> 73.7 us (0.945)
  the two profiles are of different devices: /device:TPU:32 before, /device:TPU:128 now
where the time goes in v4:
time: 73.7 us; the launch traced here: 73.5 us
  Pallas kernels  71.7 us (97%)
  local copies, waits for them, and re-layouts  1.21 us (2%)
    pallas_call x1, Pallas kernels, body(): pl.pallas_call(kernel, name='mlp_block', out_shape=(vmem((TOK, QB), bf),...  71.7 us

profile of v4, /device:TPU:128, one launch (start us, length us, event | category | flops | bytes accessed | tf_op | source)
XLA Modules:
  0.0 73.5 jit_solution(10861360278186776905)
XLA Ops:
  0.6 71.7 %mlp_block.1 = (bf16[192,128]{1,0:T(8,128)(2,1)S(1)}, f32[8,128]{1,0:T(8,128)S(1)}) custom-call(bf16[192,8192]{1,0:T(8,128)(2,1)} %tok_hbm.1, bf16[128,128]{1,0:T(8,128)(2,1)} %codes_hbm.1, s32[64]{0:T(128)} %wexp_hbm.1, s32[64]{0:T(128)} %gexp_hbm.1, s32[64]{0:T(128)} %rexp_hbm.1, bf16[192,128]{1,0:T(8,128)(2,1)} %og_hbm.1), custom_call_target="tpu_custom_call" | custom-call | tf_op jit(solution)/shard_map/mlp_block/pallas_call | solution.py:386
  72.3 0.6 copy.10
  72.9 0.6 copy.11

commit v5 on v4

--- a/solution.py
+++ b/solution.py
@@ -38,10 +38,10 @@
     tok_hbm, codes_hbm, wexp_hbm, gexp_hbm, rexp_hbm, og_hbm,
     act_out, grad_out,
     tok, codes, og, wexp, gexp, rexp,
-    wbuf, dt, cod, sibin, xout, xin, zout, zin, pout, pin,
+    wbuf, dt, cod, sibin, xout, xin, zout, zin, zpair, pout, pin,
     load_sem,
     gz_s, gz_r, gx_s, gx_r, gy_s, gy_r, gc_s, gc_r,
-    sib_s, sib_r, rx_s, rx_r, rz_s, rz_r, p_s, p_r,
+    sib_s, sib_r, rx_s, rx_r, rz_s, rz_r, pair_r, p_s, p_r,
     know0, know1, know2,
 ):
     x, y, z, c = coords()
@@ -173,16 +173,8 @@
             gy(k, mod(x - d, NX), odd).start()
             gc(origin(k, odd), mod(x - d, NX), c).start()
 
-    def gather(k):
-        @pl.when(k >= 3)
-        def _():
-            arrived_x(k - 3)
-
-        @pl.when(k < 4)
-        def _():
-            arrived_z(k)
-
-    each(7, gather)
+    each(4, arrived_z)
+    each(4, arrived_x)
     for d in (4, -4):
         pl.semaphore_signal(know0, inc=1, device_id=dev(x, y, z + d, c), device_id_type=MESH)
 
@@ -217,20 +209,19 @@
     delta = og[...].astype(jnp.float32) * sig * (1.0 + pre * (1.0 - sig))
     dt[...] = delta.astype(jnp.bfloat16).T
 
-    rest = RUN - 1
-    up = zl * 2 < rest
-    top = jnp.minimum(zl, rest - 1)
-    short, long = jnp.where(up, top, rest - 1 - top), jnp.where(up, rest - 1 - top, top)
+    spot, half = zl % 4, zl // 4
+    there_half = 4 - 4 * half
+
+    def across(n, parity):
+        return there_half + 2 * jnp.where(half == 0, 1 - n, n) + parity
+
+    def beside(n):
+        last = jnp.where(spot < 2, 1 - spot, 5 - spot)
+        return zl - spot + jnp.where(n == 2, last, jnp.where(spot < 2, 3 - n, n))
 
     def place(k):
-        n = k - 1
-        both = n - (long - short)
-        far = jnp.where(both < 0, long - n, short - both // 2)
-        ahead = up ^ ((both >= 0) & (both % 2 == 1))
-        return jnp.where(n < 0, 7 - k, jnp.where(zl < rest, top + jnp.where(ahead, far, -far), n))
-
-    early = zl >= rest
-    mine_at = jnp.where(early, 7 - zl, 7)
+        far = across(k % 2, jnp.where(k < 2, 1 - zl % 2, zl % 2))
+        return jnp.where(k < 4, far, jnp.where(k < 7, beside(k - 4), zl))
 
     def sib(k, side):
         return pltpu.make_async_remote_copy(
@@ -248,6 +239,12 @@
         return pltpu.make_async_remote_copy(
             src_ref=zout.at[k], dst_ref=zin.at[zl], send_sem=rz_s.at[k], recv_sem=rz_r.at[zl],
             device_id=(group, block(x, place(k), c)), device_id_type=MESH,
+        )
+
+    def pair(k):
+        return pltpu.make_async_remote_copy(
+            src_ref=zout.at[k], dst_ref=zpair.at[k], send_sem=rz_s.at[k], recv_sem=pair_r.at[k],
+            device_id=(group, block(x, zl + 1 - 2 * (zl % 2), c)), device_id_type=MESH,
         )
 
     def rz_wait(there):
@@ -279,9 +276,21 @@
         for d in (1, 3, 2):
             rx(k, d).wait_recv()
             total += xin[k, d - 1].astype(jnp.float32)
-        zout[k] = total.astype(jnp.bfloat16)
-
-        @pl.when(place(k) != zl)
+
+        @pl.when((k == 2) | (k == 3))
+        def _():
+            pair(k - 2).wait_recv()
+            zout[k] = (total + zpair[k - 2].astype(jnp.float32)).astype(jnp.bfloat16)
+
+        @pl.when((k < 2) | (k > 3))
+        def _():
+            zout[k] = total.astype(jnp.bfloat16)
+
+        @pl.when(k < 2)
+        def _():
+            pair(k).start()
+
+        @pl.when((k > 1) & (k < 7))
         def _():
             rz(k).start()
 
@@ -310,11 +319,11 @@
 
     def over_run():
         def add_z(k, acc):
-            there = lax.rem(zl + 1 + k, RUN)
+            there = jnp.where(k < 2, across(k, zl % 2), beside(k - 2))
             rz_wait(there)
             return acc + zin[there].astype(jnp.float32)
 
-        first = lax.fori_loop(0, 7, add_z, zout[mine_at].astype(jnp.float32))
+        first = lax.fori_loop(0, 5, add_z, zout[7].astype(jnp.float32))
         recoded = jnp.clip(first * pow2(-rexp[block(x, mirror, c)]), -code_limit, code_limit)
         recoded = recoded.astype(jnp.bfloat16).astype(jnp.float32)
         pout[...] = recoded.T.reshape(16, 8, QB)
@@ -334,11 +343,8 @@
 
         over_x(k)
 
-        @pl.when(k == jnp.where(early, 7, 7))
-        def _():
-            over_run()
-
     each(8, back)
+    over_run()
 
     @pl.when(odd == 0)
     def _():
@@ -364,11 +370,15 @@
     each(8, sent8)
 
     def sent_z(k):
-        @pl.when(place(k) != zl)
+        @pl.when(k < 2)
+        def _():
+            pair(k).wait_send()
+
+        @pl.when(k > 1)
         def _():
             rz(k).wait_send()
 
-    each(8, sent_z)
+    each(7, sent_z)
     each(16, lambda k: piece(k).wait_send())
 
     def add_piece(k, acc):
@@ -395,11 +405,11 @@
             vmem((RUN, NX, 2, QB, QB), bf), vmem((QB, TOK), bf),
             vmem((RUN, 2, NX, QB, QB), bf), vmem((RUN, NX, QB, QB), bf),
             vmem((RUN, NX, QB, QB), bf), vmem((RUN, 3, QB, QB), bf),
-            vmem((RUN, QB, QB), bf), vmem((RUN, QB, QB), bf),
+            vmem((RUN, QB, QB), bf), vmem((RUN, QB, QB), bf), vmem((2, QB, QB), bf),
             vmem((16, 8, QB), f32), vmem((16, 8, QB), f32),
             dma((6,)),
             dma((7,)), dma((4,)), dma((4, 3)), dma((4, 3)), dma((4, 4)), dma((4, 4)), dma((8, 4)), dma((8, 4)),
-            dma((8,)), dma((8,)), dma((8, 3)), dma((8, 3)), dma((8,)), dma((8,)), dma((16,)), dma((16,)),
+            dma((8,)), dma((8,)), dma((8, 3)), dma((8, 3)), dma((8,)), dma((8,)), dma((2,)), dma((16,)), dma((16,)),
             pltpu.SemaphoreType.REGULAR, pltpu.SemaphoreType.REGULAR, pltpu.SemaphoreType.REGULAR,
         ],
         compiler_params=pltpu.CompilerParams(

time: 73.7 us -> 72.3 us (0.981)
  the two profiles are of different devices: /device:TPU:128 before, /device:TPU:1 now
where the time goes in v5:
time: 72.3 us; the launch traced here: 71.8 us
  Pallas kernels  69.9 us (97%)
  local copies, waits for them, and re-layouts  1.21 us (2%)
    pallas_call x1, Pallas kernels, body(): pl.pallas_call(kernel, name='mlp_block', out_shape=(vmem((TOK, QB), bf),...  69.9 us

profile of v5, /device:TPU:1, one launch (start us, length us, event | category | flops | bytes accessed | tf_op | source)
XLA Modules:
  0.0 71.8 jit_solution(14788488119419569492)
XLA Ops:
  0.6 69.9 %mlp_block.1 = (bf16[192,128]{1,0:T(8,128)(2,1)S(1)}, f32[8,128]{1,0:T(8,128)S(1)}) custom-call(bf16[192,8192]{1,0:T(8,128)(2,1)} %tok_hbm.1, bf16[128,128]{1,0:T(8,128)(2,1)} %codes_hbm.1, s32[64]{0:T(128)} %wexp_hbm.1, s32[64]{0:T(128)} %gexp_hbm.1, s32[64]{0:T(128)} %rexp_hbm.1, bf16[192,128]{1,0:T(8,128)(2,1)} %og_hbm.1), custom_call_target="tpu_custom_call" | custom-call | tf_op jit(solution)/shard_map/mlp_block/pallas_call | solution.py:396
  70.5 0.6 copy.10
  71.2 0.6 copy.11

commit v6 on v5

--- a/solution.py
+++ b/solution.py
@@ -173,8 +173,10 @@
             gy(k, mod(x - d, NX), odd).start()
             gc(origin(k, odd), mod(x - d, NX), c).start()
 
-    each(4, arrived_z)
-    each(4, arrived_x)
+    for k in range(4):
+        arrived_z(jnp.int32(k))
+    for k in range(4):
+        arrived_x(jnp.int32(k))
     for d in (4, -4):
         pl.semaphore_signal(know0, inc=1, device_id=dev(x, y, z + d, c), device_id_type=MESH)
 
@@ -328,7 +330,8 @@
         recoded = recoded.astype(jnp.bfloat16).astype(jnp.float32)
         pout[...] = recoded.T.reshape(16, 8, QB)
         pl.semaphore_wait(know2, 2)
-        each(16, lambda k: piece(k).start())
+        for k in range(16):
+            piece(k).start()
 
     def back(k):
         @pl.when(k == 0)

time: 72.3 us -> 72 us (level)
  no operation moved by 1% of the time
where the time goes in v6:
time: 72 us; the launch traced here: 71.7 us
  Pallas kernels  69.9 us (97%)
  local copies, waits for them, and re-layouts  1.21 us (2%)
    pallas_call x1, Pallas kernels, body(): pl.pallas_call(kernel, name='mlp_block', out_shape=(vmem((TOK, QB), bf),...  69.9 us

profile of v6, /device:TPU:1, one launch (start us, length us, event | category | flops | bytes accessed | tf_op | source)
XLA Modules:
  0.0 71.7 jit_solution(6450772095642517054)
XLA Ops:
  0.6 69.9 %mlp_block.1 = (bf16[192,128]{1,0:T(8,128)(2,1)S(1)}, f32[8,128]{1,0:T(8,128)S(1)}) custom-call(bf16[192,8192]{1,0:T(8,128)(2,1)} %tok_hbm.1, bf16[128,128]{1,0:T(8,128)(2,1)} %codes_hbm.1, s32[64]{0:T(128)} %wexp_hbm.1, s32[64]{0:T(128)} %gexp_hbm.1, s32[64]{0:T(128)} %rexp_hbm.1, bf16[192,128]{1,0:T(8,128)(2,1)} %og_hbm.1), custom_call_target="tpu_custom_call" | custom-call | tf_op jit(solution)/shard_map/mlp_block/pallas_call | solution.py:399
  70.5 0.6 copy.10
  71.2 0.6 copy.11
